TPU v7x, 128 devices: a whole 4x4x4 slice. The times are simulated.
128 devices in a mesh: seq: 8 (over x, core), head: 16 (over z, y).
Axes of the slice: x: 4, y: 4, z: 4, core: 2. Of those that a mesh axis runs over, the one named last changes fastest.
Arguments:
- tokens: bfloat16 [16384, 2880], P(('seq', 'head')), may hold values from -6 to 6
- grad_out: bfloat16 [16384, 2880], P(('seq', 'head')), may hold values from -2 to 2
- expert_ids: int32 [16384, 4], P(('seq', 'head')), may hold values from 0 to 127, all different within a row; in each aligned block of 128 rows (0 to 127, 128 to 255, ...) at most 5 rows name the same one
- router_logits: float32 [16384, 4], P(('seq', 'head')), may hold values from -8 to 300
- w_gate: bfloat16 [128, 2880, 1440], P(('seq', 'head')), may hold values from -0.109375 to 0.109375
- w_up: bfloat16 [128, 2880, 1440], P(('seq', 'head')), may hold values from -0.109375 to 0.109375
- w_down: bfloat16 [128, 1440, 2880], P(('seq', 'head')), may hold values from -0.15625 to 0.15625
Outputs:
- grad_tokens: bfloat16 [16384, 2880], P(('seq', 'head'))
- grad_logits: float32 [16384, 4], P(('seq', 'head'))
Inputs may be any that keep to these rules, and one draw needn't show every extreme that they name: `expert_ids`: each token names 4 different experts. Among the 128 tokens of one device (aligned blocks of rows) no expert is named more than 5 times, a bound that some block reaches.
All inputs are finite; a program needn't handle non-finite values.
Results may differ from a plain program's by a relative error of at most 0.0057.
Values may be sent and summed in bfloat16 or wider, within the bound.
No kernel may reach another device: no remote copies, remote signals or barrier semaphores. Data moves between devices by JAX's collectives and lax.ppermute only.
A program may use at most 128 MiB of HBM per device.

v0:
```python
import jax
import jax.numpy as jnp
from jax import lax
from jax.sharding import PartitionSpec as P

swish_scale = 1.702


def expert_math(rows_in, grads_in, gate_w, up_w, down_w):
    gate_val = jnp.einsum("nekd,edf->nekf", rows_in, gate_w, preferred_element_type=jnp.float32)
    up_val = jnp.einsum("nekd,edf->nekf", rows_in, up_w, preferred_element_type=jnp.float32)
    back_val = jnp.einsum("nekd,efd->nekf", grads_in, down_w, preferred_element_type=jnp.float32)
    sigmoid_val = jax.nn.sigmoid(swish_scale * gate_val)
    act_val = gate_val * sigmoid_val
    hidden = act_val * (up_val + 1.0)
    pair_score = jnp.sum(back_val * hidden, axis=-1).astype(jnp.bfloat16)
    d_gate = (
        back_val
        * (up_val + 1.0)
        * (sigmoid_val + swish_scale * gate_val * sigmoid_val * (1.0 - sigmoid_val))
    ).astype(jnp.bfloat16)
    d_up = (back_val * act_val).astype(jnp.bfloat16)
    pair_grad = (
        jnp.einsum("nekf,edf->nekd", d_gate, gate_w, preferred_element_type=jnp.float32)
        + jnp.einsum("nekf,edf->nekd", d_up, up_w, preferred_element_type=jnp.float32)
    ).astype(jnp.bfloat16)
    return (pair_grad, pair_score)


def body(tokens, grad_out, expert_ids, router_logits, w_gate, w_up, w_down):
    rows_dev, model_width = tokens.shape
    pick_count = expert_ids.shape[1]
    local_experts = w_gate.shape[0]
    seq_count = lax.axis_size("seq")
    head_count = lax.axis_size("head")
    devices = seq_count * head_count
    experts_all = devices * local_experts
    capacity = max(2, (5 * rows_dev * pick_count + 4 * experts_all - 1) // (4 * experts_all))
    pair_count = rows_dev * pick_count
    flat_ids = expert_ids.reshape(pair_count)
    onehot = (flat_ids[:, None] == jnp.arange(experts_all, dtype=jnp.int32)[None, :]).astype(
        jnp.int32
    )
    slot_rank = jnp.sum((jnp.cumsum(onehot, axis=0) - onehot) * onehot, axis=1)
    slot_index = flat_ids * capacity + slot_rank
    slot_owner = jnp.full((experts_all * capacity,), pair_count, jnp.int32)
    slot_owner = slot_owner.at[slot_index].set(jnp.arange(pair_count, dtype=jnp.int32))
    source_row = slot_owner // pick_count
    padded_x = jnp.concatenate([tokens, jnp.zeros((1, model_width), tokens.dtype)], axis=0)
    padded_dy = jnp.concatenate([grad_out, jnp.zeros((1, model_width), grad_out.dtype)], axis=0)
    send_shape = (devices, local_experts, capacity, model_width)
    send_x = padded_x[source_row].reshape(send_shape)
    send_dy = padded_dy[source_row].reshape(send_shape)
    grad_rows, score_rows = expert_math(
        lax.all_to_all(send_x, ("seq", "head"), split_axis=0, concat_axis=0, tiled=True),
        lax.all_to_all(send_dy, ("seq", "head"), split_axis=0, concat_axis=0, tiled=True),
        w_gate,
        w_up,
        w_down,
    )
    back_grad = lax.all_to_all(grad_rows, ("seq", "head"), split_axis=0, concat_axis=0, tiled=True)
    back_score = lax.all_to_all(
        score_rows, ("seq", "head"), split_axis=0, concat_axis=0, tiled=True
    )
    weights = jax.nn.softmax(router_logits, axis=-1)
    returned = back_grad.reshape(experts_all * capacity, model_width)[slot_index]
    returned = returned.reshape(rows_dev, pick_count, model_width).astype(jnp.float32)
    grad_tokens = jnp.sum(weights[:, :, None] * returned, axis=1).astype(jnp.bfloat16)
    scores = (
        back_score.reshape(experts_all * capacity)[slot_index]
        .reshape(rows_dev, pick_count)
        .astype(jnp.float32)
    )
    grad_logits = weights * (scores - jnp.sum(weights * scores, axis=-1, keepdims=True))
    return (grad_tokens, grad_logits)


def solution(mesh):
    in_specs = (
        P(("seq", "head"), None),
        P(("seq", "head"), None),
        P(("seq", "head"), None),
        P(("seq", "head"), None),
        P(("seq", "head"), None, None),
        P(("seq", "head"), None, None),
        P(("seq", "head"), None, None),
    )
    out_specs = (P(("seq", "head"), None), P(("seq", "head"), None))
    return jax.shard_map(body, mesh=mesh, in_specs=in_specs, out_specs=out_specs, check_vma=False)
```

profile of v0, /device:TPU:0, one launch (start us, length us, event | category | flops | bytes accessed | tf_op | source)
XLA Modules:
  0.0 378.3 jit_solution(9976830995377879201)
XLA Ops:
  0.6 0.7 broadcast_multiply_fusion
  1.3 0.8 copy.47
  2.1 0.1 eq.29
  2.2 0.1 eq.25
  2.3 1.5 copy.45
  3.8 0.1 copy.46
  3.9 0.1 mul.64
  4.0 0.1 copy.49
  4.1 0.2 fusion.35
  4.4 0.2 fusion.34
  4.7 2.4 scatter_custom_fusion
  7.2 0.1 concatenate.6
  7.2 4.6 %gather_fusion = bf16[640,2880]{1,0:T(8,128)(2,1)} fusion(bf16[129,2880]{1,0:T(8,128)(2,1)S(1)} %concatenate.6, s32[1024]{0:T(1024)S(1)} %pad_clamp_fusion.1), kind=kCustom, calls=%fused_computation | custom fusion | bytes 7375360 | tf_op jit(solution)/shard_map/gather | solution.py:53
  11.8 7.4 %reshape.116 = bf16[128,1,5,2880]{3,2,0,1:T(8,128)(2,1)} reshape(bf16[640,2880]{1,0:T(8,128)(2,1)} %gather_fusion) | data formatting | bytes 7372800 | tf_op jit(solution)/shard_map/reshape | solution.py:53
  19.2 11.6 %all-to-all-start = ((bf16[128,1,5,2880]{3,2,1,0:T(8,128)(2,1)}), bf16[128,1,5,2880]{3,2,1,0:T(8,128)(2,1)}, u32[]{:S(2)}, u32[]{:S(2)}) async-start(bf16[128,1,5,2880]{3,2,1,0:T(8,128)(2,1)} %bitcast.125), calls=%async_computation | async-start | bytes 12058624 | tf_op jit(solution)/shard_map/all_to_all | solution.py:56
  30.8 0.3 copy.53
  31.2 0.1 concatenate.7
  31.2 4.6 %gather_fusion.1 = bf16[640,2880]{1,0:T(8,128)(2,1)} fusion(bf16[129,2880]{1,0:T(8,128)(2,1)S(1)} %concatenate.7, s32[1024]{0:T(1024)S(1)} %pad_clamp_fusion.1), kind=kCustom, calls=%fused_computation.1 | custom fusion | bytes 7375360 | tf_op jit(solution)/shard_map/gather | solution.py:52
  35.8 7.4 %reshape.119 = bf16[128,1,5,2880]{3,2,0,1:T(8,128)(2,1)} reshape(bf16[640,2880]{1,0:T(8,128)(2,1)} %gather_fusion.1) | data formatting | bytes 7372800 | tf_op jit(solution)/shard_map/reshape | solution.py:52
  43.2 63.7 %all-to-all-done = bf16[128,1,5,2880]{3,2,1,0:T(8,128)(2,1)} async-done(((bf16[128,1,5,2880]{3,2,1,0:T(8,128)(2,1)}), bf16[128,1,5,2880]{3,2,1,0:T(8,128)(2,1)}, u32[]{:S(2)}, u32[]{:S(2)}) %all-to-all-start) | async-done | bytes 3686432 | tf_op jit(solution)/shard_map/all_to_all | solution.py:56
  106.9 6.0 %all-to-all-start.1 = ((bf16[128,1,5,2880]{3,2,1,0:T(8,128)(2,1)}), bf16[128,1,5,2880]{3,2,1,0:T(8,128)(2,1)}, u32[]{:S(2)}, u32[]{:S(2)}) async-start(bf16[128,1,5,2880]{3,2,1,0:T(8,128)(2,1)} %bitcast.126), calls=%async_computation.1 | async-start | bytes 12058624 | tf_op jit(solution)/shard_map/all_to_all | solution.py:55
  112.9 7.9 %copy.52 = bf16[128,1,5,2880]{0,3,2,1:T(8,128)(2,1)} copy(bf16[128,1,5,2880]{3,2,1,0:T(8,128)(2,1)} %all-to-all-done) | data formatting | bytes 7372800 | tf_op jit(solution)/shard_map/all_to_all | solution.py:56
  120.8 11.8 %fusion.8 = f32[128,5,1440]{0,2,1:T(8,128)} fusion(bf16[1,1440,2880]{2,1,0:T(8,128)(2,1)} %param.13, bf16[128,1,5,2880]{0,3,2,1:T(8,128)(2,1)} %copy.52), kind=kOutput, calls=%fused_computation.13 | convolution fusion | flops 5308416000 | bytes 15667200 | tf_op jit(solution)/shard_map/nekd,efd->nekf/dot_general | solution.py:12
  132.6 56.6 %all-to-all-done.1 = bf16[128,1,5,2880]{3,2,1,0:T(8,128)(2,1)} async-done(((bf16[128,1,5,2880]{3,2,1,0:T(8,128)(2,1)}), bf16[128,1,5,2880]{3,2,1,0:T(8,128)(2,1)}, u32[]{:S(2)}, u32[]{:S(2)}) %all-to-all-start.1) | async-done | bytes 3686432 | tf_op jit(solution)/shard_map/all_to_all | solution.py:55
  189.1 7.9 %copy.55 = bf16[128,1,5,2880]{0,3,2,1:T(8,128)(2,1)} copy(bf16[128,1,5,2880]{3,2,1,0:T(8,128)(2,1)} %all-to-all-done.1) | data formatting | bytes 7372800 | tf_op jit(solution)/shard_map/all_to_all | solution.py:55
  197.0 10.7 %fusion.2 = f32[128,5,1440]{0,2,1:T(8,128)S(1)} fusion(bf16[1,2880,1440]{1,2,0:T(8,128)(2,1)} %param.11, bf16[128,1,5,2880]{0,3,2,1:T(8,128)(2,1)} %copy.55), kind=kOutput, calls=%fused_computation.7 | convolution fusion | flops 5308416000 | bytes 15667200 | tf_op jit(solution)/shard_map/nekd,edf->nekf/dot_general | solution.py:10
  207.7 0.0 slice-start.2
  207.7 12.9 %fusion.18 = (bf16[128,5]{0,1:T(8,128)(2,1)S(1)}, f32[128,5,1440]{0,2,1:T(8,128)}) fusion(f32[128,5,1440]{0,2,1:T(8,128)S(1)} %copy-done.3, f32[128,5,1440]{0,2,1:T(8,128)S(1)} %fusion.2, bf16[128,1,5,2880]{0,3,2,1:T(8,128)(2,1)S(1)} %copy-done, bf16[1,2880,1440]{1,2,0:T(8,128)(2,1)} %param.12), kind=kOutput, calls=%fused_computation.23 | convolution fusion | flops 5316709888 | bytes 23041280 | tf_op jit(solution)/shard_map/nekd,edf->nekf/dot_general | solution.py:11
  220.6 13.8 %fusion = f32[128,5,2880]{0,2,1:T(8,128)} fusion(bf16[1,2880,1440]{1,2,0:T(8,128)(2,1)S(1)} %bitcast.135, f32[128,5,1440]{0,2,1:T(8,128)} %get-tuple-element.11, f32[128,5,1440]{0,2,1:T(8,128)S(1)} %copy-done.3, f32[128,5,1440]{0,2,1:T(8,128)} %copy-done.4), kind=kOutput, calls=%fused_computation.5 | convolution fusion | flops 5318553600 | bytes 26726400 | tf_op jit(solution)/shard_map/nekf,edf->nekd/dot_general | solution.py:24
  234.5 0.8 copy.57
  235.2 4.6 %all-to-all-start.3 = ((bf16[128,1,5]{2,1,0:T(2,128)(2,1)}), bf16[128,1,5]{2,1,0:T(2,128)(2,1)S(1)}, u32[]{:S(2)}, u32[]{:S(2)}) async-start(bf16[128,1,5]{2,1,0:T(2,128)(2,1)} %copy.57), calls=%async_computation.3 | async-start | bytes 131072 | tf_op jit(solution)/shard_map/all_to_all | solution.py:62
  239.8 14.8 %fusion.12 = bf16[128,1,5,2880]{0,3,2,1:T(8,128)(2,1)} fusion(f32[128,5,2880]{0,2,1:T(8,128)} %fusion, bf16[1,2880,1440]{1,2,0:T(8,128)(2,1)} %param.12, f32[128,5,1440]{0,2,1:T(8,128)} %fusion.8, f32[128,5,1440]{0,2,1:T(8,128)} %copy-done.4), kind=kOutput, calls=%fused_computation.17 | convolution fusion | flops 5318553600 | bytes 26726400 | tf_op jit(solution)/shard_map/nekf,edf->nekd/dot_general | solution.py:25
  254.6 8.3 %copy.56 = bf16[128,1,5,2880]{3,2,1,0:T(8,128)(2,1)} copy(bf16[128,1,5,2880]{0,3,2,1:T(8,128)(2,1)} %fusion.12) | data formatting | bytes 7372800 | tf_op jit(solution)/shard_map/convert_element_type | solution.py:26
  262.9 0.0 all-to-all-done.3
  262.9 10.5 %all-to-all-start.2 = ((bf16[128,1,5,2880]{3,2,1,0:T(8,128)(2,1)}), bf16[128,1,5,2880]{3,2,1,0:T(8,128)(2,1)}, u32[]{:S(2)}, u32[]{:S(2)}) async-start(bf16[128,1,5,2880]{3,2,1,0:T(8,128)(2,1)} %copy.56), calls=%async_computation.2 | async-start | bytes 12058624 | tf_op jit(solution)/shard_map/all_to_all | solution.py:61
  273.5 0.2 reduce.1
  273.7 0.2 reshape.126
  273.9 3.5 gather_fusion.3
  277.4 0.1 reshape.128
  277.5 0.1 copy.59
  277.6 0.1 copy.44
  277.7 0.6 subtract_multiply_fusion
  278.3 71.4 %all-to-all-done.2 = bf16[128,1,5,2880]{3,2,1,0:T(8,128)(2,1)} async-done(((bf16[128,1,5,2880]{3,2,1,0:T(8,128)(2,1)}), bf16[128,1,5,2880]{3,2,1,0:T(8,128)(2,1)}, u32[]{:S(2)}, u32[]{:S(2)}) %all-to-all-start.2) | async-done | bytes 3686432 | tf_op jit(solution)/shard_map/all_to_all | solution.py:61
  349.7 8.0 %reshape.125 = bf16[640,2880]{1,0:T(8,128)(2,1)} reshape(bf16[128,1,5,2880]{3,2,1,0:T(8,128)(2,1)} %all-to-all-done.2) | data formatting | bytes 7372800 | tf_op jit(solution)/shard_map/reshape | solution.py:66
  357.7 8.4 %gather_fusion.2 = bf16[512,2880]{1,0:T(8,128)(2,1)S(1)} fusion(bf16[640,2880]{1,0:T(8,128)(2,1)} %reshape.125, s32[1024]{0:T(1024)S(1)} %pad_clamp_fusion), kind=kCustom, calls=%fused_computation.2 | custom fusion | bytes 5900288 | tf_op jit(solution)/shard_map/gather | solution.py:66
  366.1 3.6 reshape.127
  369.6 7.1 %multiply_reduce_fusion = bf16[128,2880]{1,0:T(8,128)(2,1)S(1)} fusion(f32[128,4,2880]{2,1,0:T(4,128)} %reshape.127, f32[128,4]{1,0:T(8,128)S(1)} %copy.44), kind=kLoop, calls=%fused_computation.16 | loop fusion | flops 2580480 | bytes 6637568 | tf_op jit(solution)/shard_map/reduce_sum | solution.py:68
  376.7 1.1 copy.60
  (30 shorter events, 0.2 us)
Async XLA Ops:
  19.2 11.6 %copy-start.1 = (bf16[128,2880]{0,1:T(8,128)(2,1)S(1)}, bf16[128,2880]{0,1:T(8,128)(2,1)}, u32[]{:S(2)}) copy-start(bf16[128,2880]{0,1:T(8,128)(2,1)} %param.7) | copy-start | bytes 2211844
  19.2 87.7 %all-to-all-start = ((bf16[128,1,5,2880]{3,2,1,0:T(8,128)(2,1)}), bf16[128,1,5,2880]{3,2,1,0:T(8,128)(2,1)}, u32[]{:S(2)}, u32[]{:S(2)}) async-start(bf16[128,1,5,2880]{3,2,1,0:T(8,128)(2,1)} %bitcast.125), calls=%async_computation | async-start | bytes 12058624 | tf_op jit(solution)/shard_map/all_to_all | solution.py:56
  106.9 82.2 %all-to-all-start.1 = ((bf16[128,1,5,2880]{3,2,1,0:T(8,128)(2,1)}), bf16[128,1,5,2880]{3,2,1,0:T(8,128)(2,1)}, u32[]{:S(2)}, u32[]{:S(2)}) async-start(bf16[128,1,5,2880]{3,2,1,0:T(8,128)(2,1)} %bitcast.126), calls=%async_computation.1 | async-start | bytes 12058624 | tf_op jit(solution)/shard_map/all_to_all | solution.py:55
  197.0 10.7 %copy-start = (bf16[128,1,5,2880]{0,3,2,1:T(8,128)(2,1)S(1)}, bf16[128,1,5,2880]{0,3,2,1:T(8,128)(2,1)}, u32[]{:S(2)}) copy-start(bf16[128,1,5,2880]{0,3,2,1:T(8,128)(2,1)} %copy.55) | copy-start | bytes 11059204
  197.0 10.7 %copy-start.3 = (f32[128,5,1440]{0,2,1:T(8,128)S(1)}, f32[128,5,1440]{0,2,1:T(8,128)}, u32[]{:S(2)}) copy-start(f32[128,5,1440]{0,2,1:T(8,128)} %fusion.8) | copy-start | bytes 11059204
  197.0 23.6 %slice-start = ((s8[8478720]{0:T(1024)(128)(4,1)}), s8[4194304]{0:T(1024)(128)(4,1)S(1)}, s32[]{:S(2)}) async-start(s8[8478720]{0:T(1024)(128)(4,1)} %bitcast.134), calls=%async_computation.4 | async-start | bytes 8388608
  197.0 23.6 %slice-start.1 = ((s8[8478720]{0:T(1024)(128)(4,1)}), s8[4194304]{0:T(1024)(128)(4,1)S(1)}, s32[]{:S(2)}) async-start(s8[8478720]{0:T(1024)(128)(4,1)} %bitcast.134), calls=%async_computation.5 | async-start | bytes 8388608
  207.7 12.9 %copy-start.4 = (f32[128,5,1440]{0,2,1:T(8,128)}, f32[128,5,1440]{0,2,1:T(8,128)S(1)}, u32[]{:S(2)}) copy-start(f32[128,5,1440]{0,2,1:T(8,128)S(1)} %fusion.2) | copy-start | bytes 11059204
  207.7 12.9 %slice-start.2 = ((s8[8478720]{0:T(1024)(128)(4,1)}), s8[90112]{0:T(1024)(128)(4,1)S(1)}, s32[]{:S(2)}) async-start(s8[8478720]{0:T(1024)(128)(4,1)} %bitcast.134), calls=%async_computation.6 | async-start | bytes 180224
  235.2 27.7 %all-to-all-start.3 = ((bf16[128,1,5]{2,1,0:T(2,128)(2,1)}), bf16[128,1,5]{2,1,0:T(2,128)(2,1)S(1)}, u32[]{:S(2)}, u32[]{:S(2)}) async-start(bf16[128,1,5]{2,1,0:T(2,128)(2,1)} %copy.57), calls=%async_computation.3 | async-start | bytes 131072 | tf_op jit(solution)/shard_map/all_to_all | solution.py:62
  262.9 10.5 %copy-start.2 = (f32[128,4]{0,1:T(4,128)S(1)}, f32[128,4]{0,1:T(4,128)}, u32[]{:S(2)}) copy-start(f32[128,4]{0,1:T(4,128)} %param.10) | copy-start | bytes 6148
  262.9 86.8 %all-to-all-start.2 = ((bf16[128,1,5,2880]{3,2,1,0:T(8,128)(2,1)}), bf16[128,1,5,2880]{3,2,1,0:T(8,128)(2,1)}, u32[]{:S(2)}, u32[]{:S(2)}) async-start(bf16[128,1,5,2880]{3,2,1,0:T(8,128)(2,1)} %copy.56), calls=%async_computation.2 | async-start | bytes 12058624 | tf_op jit(solution)/shard_map/all_to_all | solution.py:61
where the time goes:
time: 385 us; the launch traced here: 378 us
  waiting for transfers between devices  192 us (50%)
  local copies, waits for them, and re-layouts  79.5 us (21%)
  matrix products  63.9 us (17%)
  starting transfers between devices  32.7 us (8%)
  other arithmetic  9.13 us (2%)
    all_to_all x1, waiting for transfers between devices, body(): lax.all_to_all(grad_rows, ('seq', 'head'), split_axis=0, concat_axis=0, t...  71.4 us
    all_to_all x1, waiting for transfers between devices, body(): lax.all_to_all(send_dy, ('seq', 'head'), split_axis=0, concat_axis=0, til...  63.7 us
    all_to_all x1, waiting for transfers between devices, body(): lax.all_to_all(send_x, ('seq', 'head'), split_axis=0, concat_axis=0, tile...  56.6 us
    dot_general x1, matrix products, expert_math(): jnp.einsum('nekf,edf->nekd', d_up, up_w, preferred_element_type=jnp.float32)  14.8 us
    dot_general x1, matrix products, expert_math(): jnp.einsum('nekf,edf->nekd', d_gate, gate_w, preferred_element_type=jnp.f...  13.8 us
    dot_general x1, matrix products, expert_math(): jnp.einsum('nekd,edf->nekf', rows_in, up_w, preferred_element_type=jnp.fl...  12.9 us
    dot_general x1, matrix products, expert_math(): jnp.einsum('nekd,efd->nekf', grads_in, down_w, preferred_element_type=jnp...  11.8 us
    all_to_all x1, starting transfers between devices, body(): lax.all_to_all(send_dy, ('seq', 'head'), split_axis=0, concat_axis=0, til...  11.6 us
  transfers between devices with their start and end apart: 4, of which 3 were waited for; matrix products, arithmetic and copies ran while one was open for 16% of the time, Pallas kernels for 0%

commit v1 on v0

v1 whole, which is shorter than its diff:
```python
import jax
import jax.numpy as jnp
from jax import lax
from jax.experimental import pallas as pl
from jax.experimental.pallas import tpu as pltpu
from jax.sharding import PartitionSpec as P

swish_scale = 1.702

D = 2880
FF = 1440
TOP = 4
TOK = 128
EXP = 128
CAP = 5
ROWS = 8
EXTRA = 2944
PIECE = 768
IN_W = EXTRA + PIECE
OUT_W = 1920
TAIL = D - OUT_W
SCORE_AT = 1024
GROUP = 32
PAIRS = GROUP * CAP
GROUPS = TOK // GROUP
F_STEP = 480
MB = 1024 * 1024
bf16 = jnp.bfloat16
f32 = jnp.float32


def iota(shape, dim):
    return lax.broadcasted_iota(jnp.int32, shape, dim)


def as_bf16(mask):
    return jnp.where(mask, 1.0, 0.0).astype(bf16)


def dot_nt(a, b):
    return lax.dot_general(a, b, (((1,), (1,)), ((), ())), preferred_element_type=f32)


def dot_nn(a, b):
    return jnp.dot(a, b, preferred_element_type=f32)


def ranks_of(ids):
    expert = iota((EXP, TOK), 0)
    naming = ids[0:1, :] == expert
    for k in range(1, TOP):
        naming = jnp.logical_or(naming, ids[k : k + 1, :] == expert)
    before = as_bf16(iota((TOK, TOK), 0) < iota((TOK, TOK), 1))
    rank = dot_nn(as_bf16(naming), before)
    return naming, jnp.where(naming, rank, -1.0)


def dispatch_kernel(ids_ref, x_ref, dy_ref, out_ref, both, pieces):
    step = pl.program_id(0)
    rows = GROUP * ROWS

    @pl.when(step == 0)
    def _():
        both[:, 0:TOK] = x_ref[...]
        both[:, TOK : 2 * TOK] = dy_ref[...]
        for c in range(4):
            high = min(PIECE, D - c * PIECE)
            pieces[0:high, c * TOK : (c + 1) * TOK] = dy_ref[c * PIECE : c * PIECE + high, :]
            if high < PIECE:
                pieces[high:PIECE, c * TOK : (c + 1) * TOK] = jnp.zeros((PIECE - high, TOK), bf16)

    _, rank = ranks_of(ids_ref[...])
    spread = as_bf16(iota((rows, EXP), 1) == step * GROUP + (iota((rows, EXP), 0) >> 3))
    slot = dot_nn(spread, rank.astype(bf16)).astype(jnp.int32)
    q = iota((rows, TOK), 0) & 7
    pick_x = as_bf16(jnp.logical_and(slot == q, q < CAP))
    pick_dy = as_bf16(jnp.logical_and(slot == q - CAP, q >= CAP))
    out_ref[:, 0:D] = dot_nt(jnp.concatenate([pick_x, pick_dy], axis=1), both[...]).astype(bf16)
    out_ref[:, D:EXTRA] = jnp.zeros((rows, EXTRA - D), bf16)
    late = slot == 3 + (q >> 2)
    pick = [as_bf16(jnp.logical_and(late, (q & 3) == c)) for c in range(4)]
    out_ref[:, EXTRA:IN_W] = dot_nt(jnp.concatenate(pick, axis=1), pieces[...]).astype(bf16)


def dispatch(ids, x, dy):
    whole = lambda shape: pl.BlockSpec(shape, lambda i: (0, 0))
    return pl.pallas_call(
        dispatch_kernel,
        grid=(GROUPS,),
        out_shape=jax.ShapeDtypeStruct((EXP * ROWS, IN_W), bf16),
        in_specs=[whole((TOP, TOK)), whole((D, TOK)), whole((D, TOK))],
        out_specs=pl.BlockSpec((GROUP * ROWS, IN_W), lambda i: (i, 0)),
        scratch_shapes=[pltpu.VMEM((D, 2 * TOK), bf16), pltpu.VMEM((PIECE, 4 * TOK), bf16)],
        compiler_params=pltpu.CompilerParams(vmem_limit_bytes=40 * MB),
        cost_estimate=pl.CostEstimate(flops=2 * 1024 * 256 * 4400, bytes_accessed=10 * MB, transcendentals=0),
        name="dispatch",
    )(ids, x, dy)


def expert_kernel(wire_ref, gate_ref, up_ref, down_ref, out_ref, x_all, dy_all, total, score):
    step = pl.program_id(0)
    rows = GROUP * ROWS

    @pl.when(step == 0)
    def _():
        r, c = iota((rows, rows), 0), iota((rows, rows), 1)
        main = as_bf16(c == (r & 31) * ROWS + (r >> 5))
        late = as_bf16(c == (r & 31) * ROWS + ((r >> 5) & 1) * 4 + (r >> 6))
        for g in range(GROUPS):
            at, to = g * rows, g * PAIRS
            front = dot_nn(main, wire_ref[at : at + rows, 0:D]).astype(bf16)
            x_all[to : to + PAIRS, :] = front[0:PAIRS]
            dy_all[to : to + 96, :] = front[PAIRS:rows]
            rest = dot_nn(late, wire_ref[at : at + rows, EXTRA:IN_W]).astype(bf16)
            for p in range(4):
                high = min(PIECE, D - p * PIECE)
                dy_all[to + 96 : to + PAIRS, p * PIECE : p * PIECE + high] = rest[p * 64 : (p + 1) * 64, 0:high]

    for h in range(2):
        part = slice(h * 320, (h + 1) * 320)
        gate = dot_nt(x_all[part, :], gate_ref[...])
        up = dot_nt(x_all[part, :], up_ref[...]) + 1.0
        back = dot_nt(dy_all[part, :], down_ref[...])
        sig = jax.nn.sigmoid(swish_scale * gate)
        act = gate * sig
        back_up = back * up
        own = jnp.sum(act * back_up, axis=1, keepdims=True)
        d_gate = (back_up * (sig + swish_scale * act * (1.0 - sig))).astype(bf16)
        d_up = (back * act).astype(bf16)
        grad = dot_nn(d_gate, gate_ref[...]) + dot_nn(d_up, up_ref[...])

        @pl.when(step == 0)
        def _():
            total[part, :] = grad
            score[part, :] = own

        @pl.when(step > 0)
        def _():
            total[part, :] += grad
            score[part, :] += own

    @pl.when(step == pl.num_programs(0) - 1)
    def _():
        r, c = iota((rows, PAIRS), 0), iota((rows, PAIRS), 1)
        q, s = r & 7, c >> 5
        same = (r >> 3) == (c & 31)
        main = as_bf16(jnp.logical_and(same, q == s))
        left = as_bf16(jnp.logical_and(same, jnp.logical_and(q >= CAP, s == 2 * (q - CAP))))
        right = as_bf16(jnp.logical_and(same, jnp.logical_and(q >= CAP, s == 2 * (q - CAP) + 1)))
        last = as_bf16(jnp.logical_and(same, q == 7))
        for g in range(GROUPS):
            at, to = g * rows, g * PAIRS
            pairs = slice(to, to + PAIRS)
            tail = jnp.concatenate([total[pairs, OUT_W:D], jnp.zeros((PAIRS, SCORE_AT - TAIL), f32)], axis=1)
            late = pltpu.roll(tail, SCORE_AT - TAIL, 1).astype(bf16)
            tail = tail.astype(bf16)
            lane, slot = iota((PAIRS, 128), 1), iota((PAIRS, 128), 0) >> 5
            marks = jnp.where(lane == slot, score[pairs, :], 0.0).astype(bf16)
            body = dot_nn(main, total[pairs, 0:OUT_W].astype(bf16))
            early = dot_nn(left, tail)
            late = dot_nn(right, late)
            marks = dot_nn(last, marks)
            out_ref[at : at + rows, 0:896] = (body[:, 0:896] + early[:, 0:896]).astype(bf16)
            out_ref[at : at + rows, 896:1024] = (body[:, 896:1024] + early[:, 896:1024] + late[:, 0:128]).astype(bf16)
            out_ref[at : at + rows, 1024:1152] = (body[:, 1024:1152] + late[:, 128:256] + marks).astype(bf16)
            out_ref[at : at + rows, 1152:OUT_W] = (body[:, 1152:OUT_W] + late[:, 256:1024]).astype(bf16)


def experts(wire, gate_w, up_w, down_w):
    weights = pl.BlockSpec((F_STEP, D), lambda i: (i, 0))
    return pl.pallas_call(
        expert_kernel,
        grid=(FF // F_STEP,),
        out_shape=jax.ShapeDtypeStruct((TOK * ROWS, OUT_W), bf16),
        in_specs=[pl.BlockSpec((TOK * ROWS, IN_W), lambda i: (0, 0)), weights, weights, weights],
        out_specs=pl.BlockSpec((TOK * ROWS, OUT_W), lambda i: (0, 0)),
        scratch_shapes=[
            pltpu.VMEM((GROUPS * PAIRS, D), bf16),
            pltpu.VMEM((GROUPS * PAIRS, D), bf16),
            pltpu.VMEM((GROUPS * PAIRS, D), f32),
            pltpu.VMEM((GROUPS * PAIRS, 1), f32),
        ],
        compiler_params=pltpu.CompilerParams(vmem_limit_bytes=60 * MB),
        cost_estimate=pl.CostEstimate(flops=2 * 640 * 5 * D * FF, bytes_accessed=37 * MB, transcendentals=640 * FF),
        name="experts",
    )(wire, gate_w, up_w, down_w)


def combine_kernel(ids_ref, logits_ref, wire_ref, tokens_ref, logits_out_ref):
    ids = ids_ref[...]
    logits = logits_ref[...]
    scaled = jnp.exp(logits - jnp.max(logits, axis=0, keepdims=True))
    weights = scaled / jnp.sum(scaled, axis=0, keepdims=True)
    naming, rank = ranks_of(ids)
    expert = iota((EXP, TOK), 0)
    spread_w = jnp.zeros((EXP, TOK), f32)
    for k in range(TOP):
        spread_w = spread_w + jnp.where(ids[k : k + 1, :] == expert, weights[k : k + 1, :], 0.0)

    all_rows = TOK * ROWS
    sevenths = as_bf16(iota((EXP, all_rows), 1) == iota((EXP, all_rows), 0) * ROWS + 7)
    marks = dot_nn(sevenths, wire_ref[:, SCORE_AT : SCORE_AT + 128])
    score_of = jnp.zeros((EXP, TOK), f32)
    for s in range(CAP):
        score_of = score_of + jnp.where(rank == float(s), marks[:, s : s + 1], 0.0)
    scores = [
        jnp.sum(jnp.where(ids[k : k + 1, :] == expert, score_of, 0.0), axis=0, keepdims=True) for k in range(TOP)
    ]
    mean = sum(weights[k : k + 1, :] * scores[k] for k in range(TOP))
    for k in range(TOP):
        logits_out_ref[k : k + 1, :] = weights[k : k + 1, :] * (scores[k] - mean)

    by_token = spread_w.T
    high = by_token.astype(bf16)
    low = (by_token - high.astype(f32)).astype(bf16)
    spread = as_bf16(iota((EXP, all_rows), 0) == iota((EXP, all_rows), 1) >> 3)
    wide = dot_nn(jnp.concatenate([high, low, rank.T.astype(bf16)], axis=0), spread)
    slot = wide[2 * TOK : 3 * TOK].astype(jnp.int32)
    q = iota((TOK, all_rows), 1) & 7
    late = q >= CAP

    def picked(mask):
        return [jnp.where(mask, wide[i * TOK : (i + 1) * TOK], 0.0).astype(bf16) for i in range(2)]

    main = picked(slot == q)
    left = picked(jnp.logical_and(late, slot == 2 * (q - CAP)))
    right = picked(jnp.logical_and(late, slot == 2 * (q - CAP) + 1))
    a = dot_nn(jnp.concatenate(main + left, axis=0), wire_ref[:, 0:896])
    b = dot_nn(jnp.concatenate(main + left + right, axis=0), wire_ref[:, 896:1024])
    c = dot_nn(jnp.concatenate(main + right, axis=0), wire_ref[:, 1024:OUT_W])
    pair = lambda v, i: v[2 * i * TOK : (2 * i + 1) * TOK] + v[(2 * i + 1) * TOK : (2 * i + 2) * TOK]
    front = jnp.concatenate([pair(a, 0), pair(b, 0), pair(c, 0)], axis=1)
    early = jnp.concatenate([pair(a, 1), pair(b, 1)], axis=1)
    after = pltpu.roll(jnp.concatenate([pair(b, 2), pair(c, 1)], axis=1), TAIL, 1)
    lane = iota((TOK, SCORE_AT), 1)
    tail = jnp.where(lane < TAIL, early + after, 0.0)
    for j in range(OUT_W // 128):
        tokens_ref[j * 128 : (j + 1) * 128, :] = front[:, j * 128 : (j + 1) * 128].T.astype(bf16)
    for j in range(8):
        high_row = min(128, TAIL - j * 128)
        turned = tail[:, j * 128 : (j + 1) * 128].T.astype(bf16)
        tokens_ref[OUT_W + j * 128 : OUT_W + j * 128 + high_row, :] = turned[0:high_row]


def combine(ids, logits, wire):
    return pl.pallas_call(
        combine_kernel,
        out_shape=(jax.ShapeDtypeStruct((D, TOK), bf16), jax.ShapeDtypeStruct((TOP, TOK), f32)),
        compiler_params=pltpu.CompilerParams(vmem_limit_bytes=40 * MB),
        cost_estimate=pl.CostEstimate(flops=2 * 512 * 1024 * OUT_W, bytes_accessed=5 * MB, transcendentals=512),
        name="combine",
    )(ids, logits, wire)


def exchange(wire):
    rows, width = wire.shape
    cut = wire.reshape(EXP, ROWS, width)
    return lax.all_to_all(cut, ("seq", "head"), split_axis=0, concat_axis=0, tiled=True).reshape(rows, width)


def body(tokens, grad_out, expert_ids, router_logits, w_gate, w_up, w_down):
    ids = expert_ids.T
    there = exchange(dispatch(ids, tokens.T, grad_out.T))
    back = exchange(experts(there, w_gate[0].T, w_up[0].T, w_down[0]))
    grad_tokens, grad_logits = combine(ids, router_logits.T, back)
    return grad_tokens.T, grad_logits.T


def solution(mesh):
    rows = P(("seq", "head"), None)
    slabs = P(("seq", "head"), None, None)
    return jax.shard_map(
        body,
        mesh=mesh,
        in_specs=(rows, rows, rows, rows, slabs, slabs, slabs),
        out_specs=(rows, rows),
        check_vma=False,
    )
```

time: 385 us -> 215 us (0.56); the launches traced: 378 us -> 215 us
  waiting for transfers between devices: 192 us -> 0 us
  blocking collectives: 0 us -> 154 us
  local copies, waits for them, and re-layouts: 79.5 us -> 2.91 us
  matrix products: 63.9 us -> 0 us
  Pallas kernels: 0 us -> 56.9 us
  starting transfers between devices: 32.7 us -> 0 us
  other arithmetic: 9.13 us -> 0 us
    all_to_all x4 -> x0, waiting for transfers between devices: 192 us -> none  [the longest x1 71.4 us: body(): lax.all_to_all(grad_rows, ('seq', 'head'), split_axis=0, concat_axis=0, t...]
    all_to_all x0 -> x2, blocking collectives: none -> 154 us  [exchange(): lax.all_to_all(cut, ('seq', 'head'), split_axis=0, concat_axis=0, tiled=T...]
    dot_general x5 -> x0, matrix products: 63.9 us -> none  [the longest x1 14.8 us: expert_math(): jnp.einsum('nekf,edf->nekd', d_up, up_w, preferred_element_type=jnp.float32)]
    pallas_call x0 -> x3, Pallas kernels: none -> 56.9 us  [the longest x1 47.9 us: experts(): pl.pallas_call(expert_kernel, grid=(FF // F_STEP,), out_shape=jax.ShapeDt...]
    all_to_all x4 -> x0, starting transfers between devices: 32.7 us -> none  [the longest x1 11.6 us: body(): lax.all_to_all(send_dy, ('seq', 'head'), split_axis=0, concat_axis=0, til...]
    reshape x4 -> x0, local copies, waits for them, and re-layouts: 22.9 us -> none  [the longest x1 7.96 us: body(): back_grad.reshape(experts_all * capacity, model_width)[slot_index]]
    gather x4 -> x0, local copies, waits for them, and re-layouts: 21.1 us -> none  [the longest x1 8.38 us: body(): back_grad.reshape(experts_all * capacity, model_width)[slot_index]]
    all_to_all x2 -> x0, local copies, waits for them, and re-layouts: 15.7 us -> none  [the longest x1 7.88 us: body(): lax.all_to_all(send_dy, ('seq', 'head'), split_axis=0, concat_axis=0, til...]
  transfers between devices with their start and end apart: 4 -> 0, of which waited for: 3 -> 0; matrix products, arithmetic and copies ran while one was open for 16% -> 0% of each run, Pallas kernels for 0% -> 0%
where the time goes in v1:
time: 215 us
  blocking collectives  154 us (72%)
  Pallas kernels  56.9 us (26%)
  local copies, waits for them, and re-layouts  2.91 us (1%)
    all_to_all x2, blocking collectives, exchange(): lax.all_to_all(cut, ('seq', 'head'), split_axis=0, concat_axis=0, tiled=T...  154 us
    pallas_call x1, Pallas kernels, experts(): pl.pallas_call(expert_kernel, grid=(FF // F_STEP,), out_shape=jax.ShapeDt...  47.9 us
    pallas_call x1, Pallas kernels, dispatch(): pl.pallas_call(dispatch_kernel, grid=(GROUPS,), out_shape=jax.ShapeDtypeS...  4.64 us
    pallas_call x1, Pallas kernels, combine(): pl.pallas_call(combine_kernel, out_shape=(jax.ShapeDtypeStruct((D, TOK),...  4.4 us

profile of v1, /device:TPU:0, one launch (start us, length us, event | category | flops | bytes accessed | tf_op | source)
XLA Modules:
  0.0 214.6 jit_solution(18017827041326413415)
XLA Ops:
  0.6 0.0 copy-start
  0.6 1.1 copy-done
  1.7 0.0 copy-start.1
  1.7 1.1 copy-done.1
  2.9 0.0 copy-start.2
  2.9 0.7 copy-done.2
  3.5 4.6 %dispatch.1 = bf16[1024,3712]{1,0:T(8,128)(2,1)S(1)} custom-call(s32[4,128]{1,0:T(4,128)S(1)} %bitcast.21, bf16[2880,128]{1,0:T(8,128)(2,1)S(1)} %bitcast.19, bf16[2880,128]{1,0:T(8,128)(2,1)S(1)} %bitcast.20), custom_call_target="tpu_custom_call" | custom-call | flops 2306867200 | bytes 10485760 | tf_op jit(solution)/shard_map/dispatch/pallas_call | solution.py:87
  8.2 99.6 %all_to_all.10 = bf16[128,8,3712]{2,1,0:T(8,128)(2,1)} all-to-all(bf16[128,8,3712]{2,1,0:T(8,128)(2,1)S(1)} %bitcast.17), channel_id=1, replica_groups=mesh['seq'=8,'head'=16] {'seq','head'}, dimensions={0} | all-to-all | bytes 15204352 | tf_op jit(solution)/shard_map/all_to_all | solution.py:258
  107.8 47.9 %experts.1 = bf16[1024,1920]{1,0:T(8,128)(2,1)} custom-call(bf16[1024,3712]{1,0:T(8,128)(2,1)} %bitcast.24, bf16[1440,2880]{1,0:T(8,128)(2,1)} %bitcast.26, bf16[1440,2880]{1,0:T(8,128)(2,1)} %bitcast.27, bf16[1440,2880]{1,0:T(8,128)(2,1)} %bitcast.28), custom_call_target="tpu_custom_call" | custom-call | flops 26542080000 | bytes 38797312 | tf_op jit(solution)/shard_map/experts/pallas_call | solution.py:171
  155.7 0.0 copy-start.3
  155.7 0.0 copy-start.4
  155.7 54.5 %all_to_all.11 = bf16[128,8,1920]{2,1,0:T(8,128)(2,1)S(1)} all-to-all(bf16[128,8,1920]{2,1,0:T(8,128)(2,1)} %bitcast.25), channel_id=1, replica_groups=mesh['seq'=8,'head'=16] {'seq','head'}, dimensions={0} | all-to-all | bytes 7864320 | tf_op jit(solution)/shard_map/all_to_all | solution.py:258
  210.2 0.0 copy-done.3
  210.2 0.0 copy-done.4
  210.2 4.4 %combine.1 = (bf16[2880,128]{1,0:T(8,128)(2,1)}, f32[4,128]{1,0:T(4,128)}) custom-call(s32[4,128]{1,0:T(4,128)S(1)} %bitcast.22, f32[4,128]{1,0:T(4,128)S(1)} %bitcast.23, bf16[1024,1920]{1,0:T(8,128)(2,1)S(1)} %bitcast.18), custom_call_target="tpu_custom_call" | custom-call | flops 2013265920 | bytes 5242880 | tf_op jit(solution)/shard_map/combine/pallas_call | solution.py:246
Async XLA Ops:
  0.6 1.1 copy-start
  1.7 1.1 copy-start.1
  2.9 0.7 copy-start.2
  155.7 54.5 %copy-start.3 = (s32[128,4]{0,1:T(4,128)S(1)}, s32[128,4]{0,1:T(4,128)}, u32[]{:S(2)}) copy-start(s32[128,4]{0,1:T(4,128)} %param.9) | copy-start | bytes 6148
  155.7 54.5 %copy-start.4 = (f32[128,4]{0,1:T(4,128)S(1)}, f32[128,4]{0,1:T(4,128)}, u32[]{:S(2)}) copy-start(f32[128,4]{0,1:T(4,128)} %param.10) | copy-start | bytes 6148

commit v2 on v1

v2 whole, which is shorter than its diff:
```python
import jax
import jax.numpy as jnp
from jax import lax
from jax.experimental import pallas as pl
from jax.experimental.pallas import tpu as pltpu
from jax.sharding import PartitionSpec as P

swish_scale = 1.702

D = 2880
FF = 1440
TOP = 4
TOK = 128
EXP = 128
CAP = 5
ROWS = 8
EXTRA = 2944
PIECE = 768
IN_W = EXTRA + PIECE
OUT_W = 1920
TAIL = D - OUT_W
RIGHT = 1024
SCORE_AT = 1280
GROUP = 32
PAIRS = GROUP * CAP
GROUPS = TOK // GROUP
def parts_of(total, width):
    return [(start, min(width, total - start)) for start in range(0, total, width)]


F_PARTS = parts_of(FF, 256)
D_PARTS = parts_of(D, 512)
VMEM_MB = 24
SEND_STEPS, SEND_MB = 2, 24
MB = 1024 * 1024
bf16 = jnp.bfloat16
f32 = jnp.float32


def iota(shape, dim):
    return lax.broadcasted_iota(jnp.int32, shape, dim)


def as_bf16(mask):
    return jnp.where(mask, 1.0, 0.0).astype(bf16)


def dot_nt(a, b):
    return lax.dot_general(a, b, (((1,), (1,)), ((), ())), preferred_element_type=f32)


def dot_nn(a, b):
    return jnp.dot(a, b, preferred_element_type=f32)


def ranks_of(ids):
    expert = iota((EXP, TOK), 0)
    naming = ids[0:1, :] == expert
    for k in range(1, TOP):
        naming = jnp.logical_or(naming, ids[k : k + 1, :] == expert)
    before = as_bf16(iota((TOK, TOK), 0) < iota((TOK, TOK), 1))
    rank = dot_nn(as_bf16(naming), before)
    return naming, jnp.where(naming, rank, -1.0)


def dispatch_kernel(ids_ref, x_ref, dy_ref, weight_hbm, out_ref, weight_ref, both, pieces, sem):
    step = pl.program_id(0)
    rows = EXP // SEND_STEPS * ROWS
    keep = pltpu.make_async_copy(weight_hbm, weight_ref, sem)

    @pl.when(step == 0)
    def _():
        keep.start()
        both[:, 0:TOK] = x_ref[...]
        both[:, TOK : 2 * TOK] = dy_ref[...]
        for c in range(4):
            high = min(PIECE, D - c * PIECE)
            pieces[0:high, c * TOK : (c + 1) * TOK] = dy_ref[c * PIECE : c * PIECE + high, :]
            if high < PIECE:
                pieces[high:PIECE, c * TOK : (c + 1) * TOK] = jnp.zeros((PIECE - high, TOK), bf16)

    _, rank = ranks_of(ids_ref[...])
    spread = as_bf16(iota((rows, EXP), 1) == step * (rows // ROWS) + (iota((rows, EXP), 0) >> 3))
    slot = dot_nn(spread, rank.astype(bf16)).astype(jnp.int32)
    q = iota((rows, TOK), 0) & 7
    pick_x = as_bf16(jnp.logical_and(slot == q, q < CAP))
    pick_dy = as_bf16(jnp.logical_and(slot == q - CAP, q >= CAP))
    out_ref[:, 0:D] = dot_nt(jnp.concatenate([pick_x, pick_dy], axis=1), both[...]).astype(bf16)
    out_ref[:, D:EXTRA] = jnp.zeros((rows, EXTRA - D), bf16)
    late = slot == 3 + (q >> 2)
    pick = [as_bf16(jnp.logical_and(late, (q & 3) == c)) for c in range(4)]
    out_ref[:, EXTRA:IN_W] = dot_nt(jnp.concatenate(pick, axis=1), pieces[...]).astype(bf16)

    @pl.when(step == SEND_STEPS - 1)
    def _():
        keep.wait()


def dispatch(ids, x, dy, weight):
    whole = lambda shape: pl.BlockSpec(shape, lambda i: (0, 0))
    operands = [pltpu.with_memory_space_constraint(v, pltpu.HBM) for v in (ids, x, dy, weight)]
    return pl.pallas_call(
        dispatch_kernel,
        grid=(SEND_STEPS,),
        out_shape=(pltpu.HBM((EXP * ROWS, IN_W), bf16), pltpu.VMEM((FF, D), bf16)),
        in_specs=[whole((TOP, TOK)), whole((D, TOK)), whole((D, TOK)), pl.BlockSpec(memory_space=pl.ANY)],
        out_specs=(
            pl.BlockSpec((EXP * ROWS // SEND_STEPS, IN_W), lambda i: (i, 0)),
            pl.BlockSpec(memory_space=pltpu.VMEM),
        ),
        scratch_shapes=[
            pltpu.VMEM((D, 2 * TOK), bf16),
            pltpu.VMEM((PIECE, 4 * TOK), bf16),
            pltpu.SemaphoreType.DMA,
        ],
        compiler_params=pltpu.CompilerParams(vmem_limit_bytes=SEND_MB * MB),
        cost_estimate=pl.CostEstimate(flops=2 * 1024 * 256 * 4400, bytes_accessed=10 * MB, transcendentals=0),
        name="dispatch",
    )(*operands)


def place(slot, block):
    tail = block - OUT_W // 128
    if tail < 0:
        return slot, block
    if slot % 2 == 0:
        return CAP + slot // 2, tail
    if tail < 7:
        return CAP + slot // 2, RIGHT // 128 + tail
    return 7, RIGHT // 128 + slot // 2


def expert_kernel(wire, gate_w, up_w, down_w, out_ref, x_all, dy_all, d_gate, d_up, wide):
    rows = GROUP * ROWS
    r, c = iota((rows, rows), 0), iota((rows, rows), 1)
    main = as_bf16(c == (r & 31) * ROWS + (r >> 5))
    late = as_bf16(c == (r & 31) * ROWS + ((r >> 5) & 1) * 4 + (r >> 6))
    for g in range(GROUPS):
        to = g * PAIRS
        at = slice(g * rows, (g + 1) * rows)
        front = dot_nn(main, wire[at, 0:D]).astype(bf16)
        x_all[to : to + PAIRS, :] = front[0:PAIRS]
        dy_all[to : to + 96, :] = front[PAIRS:rows]
        rest = dot_nn(late, wire[at, EXTRA:IN_W]).astype(bf16)
        for p in range(4):
            high = min(PIECE, D - p * PIECE)
            dy_all[to + 96 : to + PAIRS, p * PIECE : p * PIECE + high] = rest[p * 64 : (p + 1) * 64, 0:high]

    score = jnp.zeros((GROUPS * PAIRS, 1), f32)
    held = None
    for j in range(len(F_PARTS) + 1):
        fresh = None
        if j < len(F_PARTS):
            start, width = F_PARTS[j]
            units = slice(start, start + width)
            fresh = (
                units,
                dot_nt(x_all[...], gate_w[units, :]),
                dot_nt(x_all[...], up_w[units, :]),
                dot_nt(dy_all[...], down_w[units, :]),
            )
        if held is not None:
            units, gate, up, back = held
            sig = jax.nn.sigmoid(swish_scale * gate)
            act = gate * sig
            back_up = back * (up + 1.0)
            score = score + jnp.sum(act * back_up, axis=1, keepdims=True)
            d_gate[:, units] = (back_up * (sig + swish_scale * act * (1.0 - sig))).astype(bf16)
            d_up[:, units] = (back * act).astype(bf16)
        held = fresh

    half = 2 * rows
    for h in range(2):
        own = slice(2 * h * PAIRS, 2 * (h + 1) * PAIRS)
        for start, width in D_PARTS:
            columns = slice(start, start + width)
            grad = dot_nn(d_gate[own, :], gate_w[:, columns]) + dot_nn(d_up[own, :], up_w[:, columns])
            if width % 128:
                grad = jnp.concatenate([grad, jnp.zeros((2 * PAIRS, 64), f32)], axis=1)
            for g in range(2):
                for s in range(CAP):
                    at = g * PAIRS + s * GROUP
                    for n in range(0, width, 128):
                        q, to = place(s, (start + n) // 128)
                        block = grad[at : at + GROUP, n : n + 128]
                        wide[to, pl.ds(g * rows + q, GROUP, stride=ROWS), :] = block
        for g in range(2):
            for s in range(CAP):
                at = (2 * h + g) * PAIRS + s * GROUP
                wide[SCORE_AT // 128 + s, pl.ds(g * rows + 7, GROUP, stride=ROWS), :] = jnp.broadcast_to(
                    score[at : at + GROUP], (GROUP, 128)
                )
        for n in range(OUT_W // 128):
            out_ref[h * half : (h + 1) * half, n * 128 : (n + 1) * 128] = wide[n].astype(bf16)


def experts(wire, gate_w, up_w, down_w):
    near = pl.BlockSpec(memory_space=pltpu.VMEM)
    operands = [pltpu.with_memory_space_constraint(v, pltpu.VMEM) for v in (wire, gate_w, up_w, down_w)]
    return pl.pallas_call(
        expert_kernel,
        out_shape=pltpu.VMEM((TOK * ROWS, OUT_W), bf16),
        in_specs=[near] * 4,
        out_specs=near,
        scratch_shapes=[
            pltpu.VMEM((GROUPS * PAIRS, D), bf16),
            pltpu.VMEM((GROUPS * PAIRS, D), bf16),
            pltpu.VMEM((GROUPS * PAIRS, FF), bf16),
            pltpu.VMEM((GROUPS * PAIRS, FF), bf16),
            pltpu.VMEM((OUT_W // 128, 2 * GROUP * ROWS, 128), f32),
        ],
        compiler_params=pltpu.CompilerParams(vmem_limit_bytes=VMEM_MB * MB),
        cost_estimate=pl.CostEstimate(flops=2 * 640 * 5 * D * FF, bytes_accessed=37 * MB, transcendentals=640 * FF),
        name="experts",
    )(*operands)


def combine_kernel(ids_ref, logits_ref, wire_ref, tokens_ref, logits_out_ref):
    ids = ids_ref[...]
    logits = logits_ref[...]
    scaled = jnp.exp(logits - jnp.max(logits, axis=0, keepdims=True))
    weights = scaled / jnp.sum(scaled, axis=0, keepdims=True)
    naming, rank = ranks_of(ids)
    expert = iota((EXP, TOK), 0)
    spread_w = jnp.zeros((EXP, TOK), f32)
    for k in range(TOP):
        spread_w = spread_w + jnp.where(ids[k : k + 1, :] == expert, weights[k : k + 1, :], 0.0)

    all_rows = TOK * ROWS
    sevenths = as_bf16(iota((EXP, all_rows), 1) == iota((EXP, all_rows), 0) * ROWS + 7)
    marks = dot_nn(sevenths, wire_ref[:, SCORE_AT:OUT_W])
    score_of = jnp.zeros((EXP, TOK), f32)
    for s in range(CAP):
        score_of = score_of + jnp.where(rank == float(s), marks[:, 128 * s : 128 * s + 1], 0.0)
    scores = [
        jnp.sum(jnp.where(ids[k : k + 1, :] == expert, score_of, 0.0), axis=0, keepdims=True) for k in range(TOP)
    ]
    mean = sum(weights[k : k + 1, :] * scores[k] for k in range(TOP))
    for k in range(TOP):
        logits_out_ref[k : k + 1, :] = weights[k : k + 1, :] * (scores[k] - mean)

    spread = as_bf16(iota((EXP, all_rows), 0) == iota((EXP, all_rows), 1) >> 3)
    wide = dot_nn(jnp.concatenate([spread_w.T, rank.T], axis=0).astype(bf16), spread)
    weight = wide[0:TOK].astype(bf16)
    slot = wide[TOK : 2 * TOK].astype(jnp.int32)
    q = iota((TOK, all_rows), 1) & 7
    late = q >= CAP

    def picked(mask):
        return jnp.where(mask, weight, jnp.zeros((), bf16))

    main = picked(slot == q)
    left = picked(jnp.logical_and(late, slot == 2 * (q - CAP)))
    right = picked(jnp.logical_and(late, slot == 2 * (q - CAP) + 1))
    ends = [
        dot_nn(picked(jnp.logical_and(q == 7, slot == 2 * i + 1)), wire_ref[:, RIGHT + 128 * i : RIGHT + 128 * (i + 1)])
        for i in range(2)
    ]
    a = dot_nn(jnp.concatenate([main, left], axis=0), wire_ref[:, 0:RIGHT])
    b = dot_nn(jnp.concatenate([main, right], axis=0), wire_ref[:, RIGHT:OUT_W])
    front = jnp.concatenate([a[0:TOK], b[0:TOK]], axis=1)
    tail = a[TOK : 2 * TOK] + jnp.concatenate([b[TOK : 2 * TOK], ends[0] + ends[1]], axis=1)
    for j in range(OUT_W // 128):
        tokens_ref[j * 128 : (j + 1) * 128, :] = front[:, j * 128 : (j + 1) * 128].T.astype(bf16)
    for j in range(8):
        high_row = min(128, TAIL - j * 128)
        turned = tail[:, j * 128 : (j + 1) * 128].T.astype(bf16)
        tokens_ref[OUT_W + j * 128 : OUT_W + j * 128 + high_row, :] = turned[0:high_row]


def combine(ids, logits, wire):
    return pl.pallas_call(
        combine_kernel,
        out_shape=(jax.ShapeDtypeStruct((D, TOK), bf16), jax.ShapeDtypeStruct((TOP, TOK), f32)),
        compiler_params=pltpu.CompilerParams(vmem_limit_bytes=20 * MB),
        cost_estimate=pl.CostEstimate(flops=2 * 512 * 1024 * OUT_W, bytes_accessed=5 * MB, transcendentals=512),
        name="combine",
    )(ids, logits, wire)


def exchange(wire):
    rows, width = wire.shape
    cut = wire.reshape(EXP, ROWS, width)
    return lax.all_to_all(cut, ("seq", "head"), split_axis=0, concat_axis=0, tiled=True).reshape(rows, width)


def body(tokens, grad_out, expert_ids, router_logits, w_gate, w_up, w_down):
    ids = expert_ids.T
    sent, down = dispatch(ids, tokens.T, grad_out.T, w_down[0])
    back = exchange(experts(exchange(sent), w_gate[0].T, w_up[0].T, down))
    grad_tokens, grad_logits = combine(ids, router_logits.T, back)
    return grad_tokens.T, grad_logits.T


def solution(mesh):
    rows = P(("seq", "head"), None)
    slabs = P(("seq", "head"), None, None)
    return jax.shard_map(
        body,
        mesh=mesh,
        in_specs=(rows, rows, rows, rows, slabs, slabs, slabs),
        out_specs=(rows, rows),
        check_vma=False,
    )
```

time: 215 us -> 202 us (0.940)
  Pallas kernels: 56.9 us -> 46.7 us
  local copies, waits for them, and re-layouts: 2.91 us -> 0.05 us
    pallas_call x2, Pallas kernels: 52.5 us -> 43.9 us  [the longest x1 34.9 us: experts(): pl.pallas_call(expert_kernel, out_shape=pltpu.VMEM((TOK * ROWS, OUT_W), b...]
    unnamed x10 -> x16, local copies, waits for them, and re-layouts: 2.91 us -> 0.05 us
where the time goes in v2:
time: 202 us
  blocking collectives  154 us (76%)
  Pallas kernels  46.7 us (23%)
    all_to_all x2, blocking collectives, exchange(): lax.all_to_all(cut, ('seq', 'head'), split_axis=0, concat_axis=0, tiled=T...  154 us
    pallas_call x1, Pallas kernels, experts(): pl.pallas_call(expert_kernel, out_shape=pltpu.VMEM((TOK * ROWS, OUT_W), b...  34.9 us
    pallas_call x1, Pallas kernels, dispatch(): pl.pallas_call(dispatch_kernel, grid=(SEND_STEPS,), out_shape=(pltpu.HBM(...  9 us

profile of v2, /device:TPU:0, one launch (start us, length us, event | category | flops | bytes accessed | tf_op | source)
XLA Modules:
  0.0 201.5 jit_solution(16750113505076457640)
XLA Ops:
  0.6 0.0 slice-start
  0.6 0.0 slice-start.1
  0.7 0.0 slice-start.3
  0.7 0.0 slice-start.4
  0.7 9.0 %dispatch.1 = (bf16[1024,3712]{1,0:T(8,128)(2,1)}, bf16[1440,2880]{1,0:T(8,128)(2,1)S(1)}) custom-call(s32[4,128]{1,0:T(4,128)} %bitcast.20, bf16[2880,128]{1,0:T(8,128)(2,1)} %bitcast.31, bf16[2880,128]{1,0:T(8,128)(2,1)} %bitcast.32, bf16[1440,2880]{1,0:T(8,128)(2,1)} %bitcast.29), custom_call_target="tpu_custom_call" | custom-call | flops 2306867200 | bytes 10485760 | tf_op jit(solution)/shard_map/dispatch/pallas_call | solution.py:102
  9.7 0.0 slice-start.2
  9.7 0.0 slice-start.5
  9.7 99.7 %all_to_all.10 = bf16[128,8,3712]{2,1,0:T(8,128)(2,1)S(1)} all-to-all(bf16[128,8,3712]{2,1,0:T(8,128)(2,1)} %bitcast.30), channel_id=1, replica_groups=mesh['seq'=8,'head'=16] {'seq','head'}, dimensions={0} | all-to-all | bytes 15204352 | tf_op jit(solution)/shard_map/all_to_all | solution.py:284
  109.4 0.0 slice-done
  109.4 0.0 slice-done.1
  109.4 0.0 slice-done.3
  109.4 0.0 slice-done.4
  109.4 0.0 slice-done.2
  109.4 0.0 slice-done.5
  109.5 0.0 copy-start
  109.5 0.0 copy-start.1
  109.5 34.9 %experts.1 = bf16[1024,1920]{1,0:T(8,128)(2,1)S(1)} custom-call(bf16[1024,3712]{1,0:T(8,128)(2,1)S(1)} %bitcast.17, bf16[1440,2880]{1,0:T(8,128)(2,1)S(1)} %bitcast.24, bf16[1440,2880]{1,0:T(8,128)(2,1)S(1)} %bitcast.27, bf16[1440,2880]{1,0:T(8,128)(2,1)S(1)} %get-tuple-element.7.down_w), custom_call_target="tpu_custom_call" | custom-call | flops 26542080000 | bytes 38797312 | tf_op jit(solution)/shard_map/experts/pallas_call | solution.py:200
  144.4 54.3 %all_to_all.11 = bf16[128,8,1920]{2,1,0:T(8,128)(2,1)S(1)} all-to-all(bf16[128,8,1920]{2,1,0:T(8,128)(2,1)S(1)} %bitcast.19), channel_id=1, replica_groups=mesh['seq'=8,'head'=16] {'seq','head'}, dimensions={0} | all-to-all | bytes 7864320 | tf_op jit(solution)/shard_map/all_to_all | solution.py:284
  198.7 0.0 copy-done
  198.7 0.0 copy-done.1
  198.7 2.9 %combine.1 = (bf16[2880,128]{1,0:T(8,128)(2,1)}, f32[4,128]{1,0:T(4,128)}) custom-call(s32[4,128]{1,0:T(4,128)S(1)} %bitcast.21, f32[4,128]{1,0:T(4,128)S(1)} %bitcast.28, bf16[1024,1920]{1,0:T(8,128)(2,1)S(1)} %bitcast.18), custom_call_target="tpu_custom_call" | custom-call | flops 2013265920 | bytes 5242880 | tf_op jit(solution)/shard_map/combine/pallas_call | solution.py:272
  (2 shorter events, 0.0 us)
Async XLA Ops:
  0.6 108.8 %slice-start = ((s8[8478720]{0:T(1024)(128)(4,1)}), s8[4194304]{0:T(1024)(128)(4,1)S(1)}, s32[]{:S(2)}) async-start(s8[8478720]{0:T(1024)(128)(4,1)} %bitcast.22), calls=%async_computation.2 | async-start | bytes 8388608
  0.6 108.8 %slice-start.1 = ((s8[8478720]{0:T(1024)(128)(4,1)}), s8[4194304]{0:T(1024)(128)(4,1)S(1)}, s32[]{:S(2)}) async-start(s8[8478720]{0:T(1024)(128)(4,1)} %bitcast.22), calls=%async_computation.3 | async-start | bytes 8388608
  0.7 108.8 %slice-start.3 = ((s8[8478720]{0:T(1024)(128)(4,1)}), s8[4194304]{0:T(1024)(128)(4,1)S(1)}, s32[]{:S(2)}) async-start(s8[8478720]{0:T(1024)(128)(4,1)} %bitcast.25), calls=%async_computation.5 | async-start | bytes 8388608
  0.7 108.8 %slice-start.4 = ((s8[8478720]{0:T(1024)(128)(4,1)}), s8[4194304]{0:T(1024)(128)(4,1)S(1)}, s32[]{:S(2)}) async-start(s8[8478720]{0:T(1024)(128)(4,1)} %bitcast.25), calls=%async_computation.6 | async-start | bytes 8388608
  9.7 99.7 %slice-start.2 = ((s8[8478720]{0:T(1024)(128)(4,1)}), s8[90112]{0:T(1024)(128)(4,1)S(1)}, s32[]{:S(2)}) async-start(s8[8478720]{0:T(1024)(128)(4,1)} %bitcast.22), calls=%async_computation.4 | async-start | bytes 180224
  9.7 99.7 %slice-start.5 = ((s8[8478720]{0:T(1024)(128)(4,1)}), s8[90112]{0:T(1024)(128)(4,1)S(1)}, s32[]{:S(2)}) async-start(s8[8478720]{0:T(1024)(128)(4,1)} %bitcast.25), calls=%async_computation.7 | async-start | bytes 180224
  109.5 89.2 %copy-start = (s32[128,4]{0,1:T(4,128)S(1)}, s32[128,4]{0,1:T(4,128)}, u32[]{:S(2)}) copy-start(s32[128,4]{0,1:T(4,128)} %param.9) | copy-start | bytes 6148
  109.5 89.2 %copy-start.1 = (f32[128,4]{0,1:T(4,128)S(1)}, f32[128,4]{0,1:T(4,128)}, u32[]{:S(2)}) copy-start(f32[128,4]{0,1:T(4,128)} %param.10) | copy-start | bytes 6148

commit v3 on v2

--- a/solution.py
+++ b/solution.py
@@ -24,14 +24,17 @@
 GROUP = 32
 PAIRS = GROUP * CAP
 GROUPS = TOK // GROUP
+
+
 def parts_of(total, width):
     return [(start, min(width, total - start)) for start in range(0, total, width)]
 
 
 F_PARTS = parts_of(FF, 256)
 D_PARTS = parts_of(D, 512)
-VMEM_MB = 24
-SEND_STEPS, SEND_MB = 2, 24
+VMEM_MB = 26
+P_PARTS = parts_of(D, PIECE)
+SEND_STEPS, SEND_MB = 4, 24
 MB = 1024 * 1024
 bf16 = jnp.bfloat16
 f32 = jnp.float32
@@ -63,58 +66,59 @@
     return naming, jnp.where(naming, rank, -1.0)
 
 
-def dispatch_kernel(ids_ref, x_ref, dy_ref, weight_hbm, out_ref, weight_ref, both, pieces, sem):
-    step = pl.program_id(0)
+def dispatch_kernel(ids_ref, x_hbm, dy_hbm, out_hbm, both, pieces, parts, in_sem, out_sem):
+    sources = [(x_hbm, both.at[:, 0:TOK]), (dy_hbm, both.at[:, TOK : 2 * TOK])]
+    for c, (start, width) in enumerate(P_PARTS):
+        lanes = slice(c * TOK, (c + 1) * TOK)
+        sources.append((dy_hbm.at[start : start + width, :], pieces.at[0:width, lanes]))
+        if width < PIECE:
+            pieces[width:PIECE, lanes] = jnp.zeros((PIECE - width, TOK), bf16)
+    fetches = [pltpu.make_async_copy(source, to, in_sem.at[n]) for n, (source, to) in enumerate(sources)]
+    for fetch in fetches:
+        fetch.start()
+
+    _, rank = ranks_of(ids_ref[...])
+    rank = rank.astype(bf16)
     rows = EXP // SEND_STEPS * ROWS
-    keep = pltpu.make_async_copy(weight_hbm, weight_ref, sem)
-
-    @pl.when(step == 0)
-    def _():
-        keep.start()
-        both[:, 0:TOK] = x_ref[...]
-        both[:, TOK : 2 * TOK] = dy_ref[...]
-        for c in range(4):
-            high = min(PIECE, D - c * PIECE)
-            pieces[0:high, c * TOK : (c + 1) * TOK] = dy_ref[c * PIECE : c * PIECE + high, :]
-            if high < PIECE:
-                pieces[high:PIECE, c * TOK : (c + 1) * TOK] = jnp.zeros((PIECE - high, TOK), bf16)
-
-    _, rank = ranks_of(ids_ref[...])
-    spread = as_bf16(iota((rows, EXP), 1) == step * (rows // ROWS) + (iota((rows, EXP), 0) >> 3))
-    slot = dot_nn(spread, rank.astype(bf16)).astype(jnp.int32)
     q = iota((rows, TOK), 0) & 7
-    pick_x = as_bf16(jnp.logical_and(slot == q, q < CAP))
-    pick_dy = as_bf16(jnp.logical_and(slot == q - CAP, q >= CAP))
-    out_ref[:, 0:D] = dot_nt(jnp.concatenate([pick_x, pick_dy], axis=1), both[...]).astype(bf16)
-    out_ref[:, D:EXTRA] = jnp.zeros((rows, EXTRA - D), bf16)
-    late = slot == 3 + (q >> 2)
-    pick = [as_bf16(jnp.logical_and(late, (q & 3) == c)) for c in range(4)]
-    out_ref[:, EXTRA:IN_W] = dot_nt(jnp.concatenate(pick, axis=1), pieces[...]).astype(bf16)
-
-    @pl.when(step == SEND_STEPS - 1)
-    def _():
-        keep.wait()
-
-
-def dispatch(ids, x, dy, weight):
-    whole = lambda shape: pl.BlockSpec(shape, lambda i: (0, 0))
-    operands = [pltpu.with_memory_space_constraint(v, pltpu.HBM) for v in (ids, x, dy, weight)]
+    picks = []
+    for n in range(SEND_STEPS):
+        spread = as_bf16(iota((rows, EXP), 1) == n * (rows // ROWS) + (iota((rows, EXP), 0) >> 3))
+        slot = dot_nn(spread, rank).astype(jnp.int32)
+        front = [jnp.logical_and(slot == q, q < CAP), jnp.logical_and(slot == q - CAP, q >= CAP)]
+        late = slot == 3 + (q >> 2)
+        rest = [jnp.logical_and(late, (q & 3) == c) for c in range(4)]
+        picks.append([jnp.concatenate([as_bf16(m) for m in masks], axis=1) for masks in (front, rest)])
+        parts[n, :, D:EXTRA] = jnp.zeros((rows, EXTRA - D), bf16)
+    for fetch in fetches:
+        fetch.wait()
+    sends = []
+    for n, (front, rest) in enumerate(picks):
+        parts[n, :, 0:D] = dot_nt(front, both[...]).astype(bf16)
+        parts[n, :, EXTRA:IN_W] = dot_nt(rest, pieces[...]).astype(bf16)
+        sends.append(pltpu.make_async_copy(parts.at[n], out_hbm.at[n * rows : (n + 1) * rows, :], out_sem.at[n]))
+        sends[n].start()
+    for send in sends:
+        send.wait()
+
+
+def dispatch(ids, x, dy):
+    anywhere = pl.BlockSpec(memory_space=pl.ANY)
+    operands = [pltpu.with_memory_space_constraint(v, pltpu.HBM) for v in (ids, x, dy)]
     return pl.pallas_call(
         dispatch_kernel,
-        grid=(SEND_STEPS,),
-        out_shape=(pltpu.HBM((EXP * ROWS, IN_W), bf16), pltpu.VMEM((FF, D), bf16)),
-        in_specs=[whole((TOP, TOK)), whole((D, TOK)), whole((D, TOK)), pl.BlockSpec(memory_space=pl.ANY)],
-        out_specs=(
-            pl.BlockSpec((EXP * ROWS // SEND_STEPS, IN_W), lambda i: (i, 0)),
-            pl.BlockSpec(memory_space=pltpu.VMEM),
-        ),
+        out_shape=pltpu.HBM((EXP * ROWS, IN_W), bf16),
+        in_specs=[pl.BlockSpec(memory_space=pltpu.VMEM), anywhere, anywhere],
+        out_specs=anywhere,
         scratch_shapes=[
             pltpu.VMEM((D, 2 * TOK), bf16),
             pltpu.VMEM((PIECE, 4 * TOK), bf16),
-            pltpu.SemaphoreType.DMA,
+            pltpu.VMEM((SEND_STEPS, EXP // SEND_STEPS * ROWS, IN_W), bf16),
+            pltpu.SemaphoreType.DMA((2 + len(P_PARTS),)),
+            pltpu.SemaphoreType.DMA((SEND_STEPS,)),
         ],
         compiler_params=pltpu.CompilerParams(vmem_limit_bytes=SEND_MB * MB),
-        cost_estimate=pl.CostEstimate(flops=2 * 1024 * 256 * 4400, bytes_accessed=10 * MB, transcendentals=0),
+        cost_estimate=pl.CostEstimate(flops=8 * 1024 * 256 * 4400, bytes_accessed=40 * MB, transcendentals=0),
         name="dispatch",
     )(*operands)
 
@@ -286,8 +290,8 @@
 
 def body(tokens, grad_out, expert_ids, router_logits, w_gate, w_up, w_down):
     ids = expert_ids.T
-    sent, down = dispatch(ids, tokens.T, grad_out.T, w_down[0])
-    back = exchange(experts(exchange(sent), w_gate[0].T, w_up[0].T, down))
+    there = exchange(dispatch(ids, tokens.T, grad_out.T))
+    back = exchange(experts(there, w_gate[0].T, w_up[0].T, w_down[0]))
     grad_tokens, grad_logits = combine(ids, router_logits.T, back)
     return grad_tokens.T, grad_logits.T
 

time: 202 us -> 200 us (0.990)
  no operation moved by 1% of the time
where the time goes in v3:
time: 200 us
  blocking collectives  154 us (77%)
  Pallas kernels  45.4 us (23%)
    all_to_all x2, blocking collectives, exchange(): lax.all_to_all(cut, ('seq', 'head'), split_axis=0, concat_axis=0, tiled=T...  154 us
    pallas_call x1, Pallas kernels, experts(): pl.pallas_call(expert_kernel, out_shape=pltpu.VMEM((TOK * ROWS, OUT_W), b...  34.9 us
    pallas_call x1, Pallas kernels, dispatch(): pl.pallas_call(dispatch_kernel, out_shape=pltpu.HBM((EXP * ROWS, IN_W), b...  7.66 us

profile of v3, /device:TPU:0, one launch (start us, length us, event | category | flops | bytes accessed | tf_op | source)
XLA Modules:
  0.0 200.1 jit_solution(10488601170846783337)
XLA Ops:
  0.6 0.0 copy-start.1
  0.6 0.0 copy-start.2
  0.7 7.7 %dispatch.1 = bf16[1024,3712]{1,0:T(8,128)(2,1)} custom-call(s32[4,128]{1,0:T(4,128)} %bitcast.23, bf16[2880,128]{1,0:T(8,128)(2,1)} %bitcast.27, bf16[2880,128]{1,0:T(8,128)(2,1)} %bitcast.28), custom_call_target="tpu_custom_call" | custom-call | flops 9227468800 | bytes 41943040 | tf_op jit(solution)/shard_map/dispatch/pallas_call | solution.py:108
  8.3 0.0 copy-start
  8.3 99.7 %all_to_all.10 = bf16[128,8,3712]{2,1,0:T(8,128)(2,1)S(1)} all-to-all(bf16[128,8,3712]{2,1,0:T(8,128)(2,1)} %bitcast.26), channel_id=1, replica_groups=mesh['seq'=8,'head'=16] {'seq','head'}, dimensions={0} | all-to-all | bytes 15204352 | tf_op jit(solution)/shard_map/all_to_all | solution.py:288
  108.0 0.0 copy-done.1
  108.0 0.0 copy-done.2
  108.0 0.0 copy-done
  108.0 34.9 %experts.1 = bf16[1024,1920]{1,0:T(8,128)(2,1)S(1)} custom-call(bf16[1024,3712]{1,0:T(8,128)(2,1)S(1)} %bitcast.17, bf16[1440,2880]{1,0:T(8,128)(2,1)S(1)} %bitcast.20, bf16[1440,2880]{1,0:T(8,128)(2,1)S(1)} %bitcast.21, bf16[1440,2880]{1,0:T(8,128)(2,1)S(1)} %bitcast.22), custom_call_target="tpu_custom_call" | custom-call | flops 26542080000 | bytes 38797312 | tf_op jit(solution)/shard_map/experts/pallas_call | solution.py:204
  142.9 0.0 copy-start.3
  142.9 0.0 copy-start.4
  143.0 54.3 %all_to_all.11 = bf16[128,8,1920]{2,1,0:T(8,128)(2,1)S(1)} all-to-all(bf16[128,8,1920]{2,1,0:T(8,128)(2,1)S(1)} %bitcast.19), channel_id=1, replica_groups=mesh['seq'=8,'head'=16] {'seq','head'}, dimensions={0} | all-to-all | bytes 7864320 | tf_op jit(solution)/shard_map/all_to_all | solution.py:288
  197.2 0.0 copy-done.3
  197.2 0.0 copy-done.4
  197.2 2.9 %combine.1 = (bf16[2880,128]{1,0:T(8,128)(2,1)}, f32[4,128]{1,0:T(4,128)}) custom-call(s32[4,128]{1,0:T(4,128)S(1)} %bitcast.24, f32[4,128]{1,0:T(4,128)S(1)} %bitcast.25, bf16[1024,1920]{1,0:T(8,128)(2,1)S(1)} %bitcast.18), custom_call_target="tpu_custom_call" | custom-call | flops 2013265920 | bytes 5242880 | tf_op jit(solution)/shard_map/combine/pallas_call | solution.py:276
Async XLA Ops:
  0.6 107.4 %copy-start.1 = (bf16[1,2880,1440]{1,2,0:T(8,128)(2,1)S(1)}, bf16[1,2880,1440]{1,2,0:T(8,128)(2,1)}, u32[]{:S(2)}) copy-start(bf16[1,2880,1440]{1,2,0:T(8,128)(2,1)} %param.12) | copy-start | bytes 24883204
  0.6 107.4 %copy-start.2 = (bf16[1,1440,2880]{2,1,0:T(8,128)(2,1)S(1)}, bf16[1,1440,2880]{2,1,0:T(8,128)(2,1)}, u32[]{:S(2)}) copy-start(bf16[1,1440,2880]{2,1,0:T(8,128)(2,1)} %param.13) | copy-start | bytes 24883204
  8.3 99.7 %copy-start = (bf16[1,2880,1440]{1,2,0:T(8,128)(2,1)S(1)}, bf16[1,2880,1440]{1,2,0:T(8,128)(2,1)}, u32[]{:S(2)}) copy-start(bf16[1,2880,1440]{1,2,0:T(8,128)(2,1)} %param.11) | copy-start | bytes 24883204
  142.9 54.3 %copy-start.3 = (s32[128,4]{0,1:T(4,128)S(1)}, s32[128,4]{0,1:T(4,128)}, u32[]{:S(2)}) copy-start(s32[128,4]{0,1:T(4,128)} %param.9) | copy-start | bytes 6148
  142.9 54.3 %copy-start.4 = (f32[128,4]{0,1:T(4,128)S(1)}, f32[128,4]{0,1:T(4,128)}, u32[]{:S(2)}) copy-start(f32[128,4]{0,1:T(4,128)} %param.10) | copy-start | bytes 6148

commit v4 on v3

--- a/solution.py
+++ b/solution.py
@@ -195,7 +195,7 @@
                     score[at : at + GROUP], (GROUP, 128)
                 )
         for n in range(OUT_W // 128):
-            out_ref[h * half : (h + 1) * half, n * 128 : (n + 1) * 128] = wide[n].astype(bf16)
+            out_ref[h * half : (h + 1) * half, n * 128 : (n + 1) * 128] = wide[n, 0:half, :].astype(bf16)
 
 
 def experts(wire, gate_w, up_w, down_w):
@@ -211,7 +211,7 @@
             pltpu.VMEM((GROUPS * PAIRS, D), bf16),
             pltpu.VMEM((GROUPS * PAIRS, FF), bf16),
             pltpu.VMEM((GROUPS * PAIRS, FF), bf16),
-            pltpu.VMEM((OUT_W // 128, 2 * GROUP * ROWS, 128), f32),
+            pltpu.VMEM((OUT_W // 128, 2 * GROUP * ROWS + ROWS, 128), f32),
         ],
         compiler_params=pltpu.CompilerParams(vmem_limit_bytes=VMEM_MB * MB),
         cost_estimate=pl.CostEstimate(flops=2 * 640 * 5 * D * FF, bytes_accessed=37 * MB, transcendentals=640 * FF),

time: 200 us -> 200 us (level)
  no operation moved by 1% of the time
where the time goes in v4:
time: 200 us
  blocking collectives  154 us (77%)
  Pallas kernels  45.4 us (23%)
    all_to_all x2, blocking collectives, exchange(): lax.all_to_all(cut, ('seq', 'head'), split_axis=0, concat_axis=0, tiled=T...  154 us
    pallas_call x1, Pallas kernels, experts(): pl.pallas_call(expert_kernel, out_shape=pltpu.VMEM((TOK * ROWS, OUT_W), b...  34.9 us
    pallas_call x1, Pallas kernels, dispatch(): pl.pallas_call(dispatch_kernel, out_shape=pltpu.HBM((EXP * ROWS, IN_W), b...  7.66 us

profile of v4, /device:TPU:0, one launch (start us, length us, event | category | flops | bytes accessed | tf_op | source)
XLA Modules:
  0.0 200.1 jit_solution(6752449777387555039)
XLA Ops:
  0.6 0.0 copy-start.1
  0.6 0.0 copy-start.2
  0.7 7.7 %dispatch.1 = bf16[1024,3712]{1,0:T(8,128)(2,1)} custom-call(s32[4,128]{1,0:T(4,128)} %bitcast.23, bf16[2880,128]{1,0:T(8,128)(2,1)} %bitcast.27, bf16[2880,128]{1,0:T(8,128)(2,1)} %bitcast.28), custom_call_target="tpu_custom_call" | custom-call | flops 9227468800 | bytes 41943040 | tf_op jit(solution)/shard_map/dispatch/pallas_call | solution.py:108
  8.3 0.0 copy-start
  8.3 99.7 %all_to_all.10 = bf16[128,8,3712]{2,1,0:T(8,128)(2,1)S(1)} all-to-all(bf16[128,8,3712]{2,1,0:T(8,128)(2,1)} %bitcast.26), channel_id=1, replica_groups=mesh['seq'=8,'head'=16] {'seq','head'}, dimensions={0} | all-to-all | bytes 15204352 | tf_op jit(solution)/shard_map/all_to_all | solution.py:288
  108.0 0.0 copy-done.1
  108.0 0.0 copy-done.2
  108.0 0.0 copy-done
  108.0 34.9 %experts.1 = bf16[1024,1920]{1,0:T(8,128)(2,1)S(1)} custom-call(bf16[1024,3712]{1,0:T(8,128)(2,1)S(1)} %bitcast.17, bf16[1440,2880]{1,0:T(8,128)(2,1)S(1)} %bitcast.20, bf16[1440,2880]{1,0:T(8,128)(2,1)S(1)} %bitcast.21, bf16[1440,2880]{1,0:T(8,128)(2,1)S(1)} %bitcast.22), custom_call_target="tpu_custom_call" | custom-call | flops 26542080000 | bytes 38797312 | tf_op jit(solution)/shard_map/experts/pallas_call | solution.py:204
  142.9 0.0 copy-start.3
  142.9 0.0 copy-start.4
  142.9 54.3 %all_to_all.11 = bf16[128,8,1920]{2,1,0:T(8,128)(2,1)S(1)} all-to-all(bf16[128,8,1920]{2,1,0:T(8,128)(2,1)S(1)} %bitcast.19), channel_id=1, replica_groups=mesh['seq'=8,'head'=16] {'seq','head'}, dimensions={0} | all-to-all | bytes 7864320 | tf_op jit(solution)/shard_map/all_to_all | solution.py:288
  197.2 0.0 copy-done.3
  197.2 0.0 copy-done.4
  197.2 2.9 %combine.1 = (bf16[2880,128]{1,0:T(8,128)(2,1)}, f32[4,128]{1,0:T(4,128)}) custom-call(s32[4,128]{1,0:T(4,128)S(1)} %bitcast.24, f32[4,128]{1,0:T(4,128)S(1)} %bitcast.25, bf16[1024,1920]{1,0:T(8,128)(2,1)S(1)} %bitcast.18), custom_call_target="tpu_custom_call" | custom-call | flops 2013265920 | bytes 5242880 | tf_op jit(solution)/shard_map/combine/pallas_call | solution.py:276
Async XLA Ops:
  0.6 107.4 %copy-start.1 = (bf16[1,2880,1440]{1,2,0:T(8,128)(2,1)S(1)}, bf16[1,2880,1440]{1,2,0:T(8,128)(2,1)}, u32[]{:S(2)}) copy-start(bf16[1,2880,1440]{1,2,0:T(8,128)(2,1)} %param.12) | copy-start | bytes 24883204
  0.6 107.4 %copy-start.2 = (bf16[1,1440,2880]{2,1,0:T(8,128)(2,1)S(1)}, bf16[1,1440,2880]{2,1,0:T(8,128)(2,1)}, u32[]{:S(2)}) copy-start(bf16[1,1440,2880]{2,1,0:T(8,128)(2,1)} %param.13) | copy-start | bytes 24883204
  8.3 99.7 %copy-start = (bf16[1,2880,1440]{1,2,0:T(8,128)(2,1)S(1)}, bf16[1,2880,1440]{1,2,0:T(8,128)(2,1)}, u32[]{:S(2)}) copy-start(bf16[1,2880,1440]{1,2,0:T(8,128)(2,1)} %param.11) | copy-start | bytes 24883204
  142.9 54.3 %copy-start.3 = (s32[128,4]{0,1:T(4,128)S(1)}, s32[128,4]{0,1:T(4,128)}, u32[]{:S(2)}) copy-start(s32[128,4]{0,1:T(4,128)} %param.9) | copy-start | bytes 6148
  142.9 54.3 %copy-start.4 = (f32[128,4]{0,1:T(4,128)S(1)}, f32[128,4]{0,1:T(4,128)}, u32[]{:S(2)}) copy-start(f32[128,4]{0,1:T(4,128)} %param.10) | copy-start | bytes 6148
